TPU v7x, 32 devices: a whole 2x2x4 slice. The times are simulated.
32 devices in a mesh: lp: 2 (over y), col: 4 (over z), row: 2 (over x), sub: 2 (over core).
Axes of the slice: x: 2, y: 2, z: 4, core: 2. Of those that a mesh axis runs over, the one named last changes fastest.
Arguments:
- matrix: bfloat16 [128, 10, 128, 128], P(('lp', 'col', 'row')), parts along dimension 0, may hold values from -0.15625 to 0.15625
- band_cols: int32 [128, 10], P(('lp', 'col', 'row')), parts along dimension 0, may hold values from 0 to 7, as said below
- x_start: float32 [2048, 256], P(('lp', 'col', 'row'), 'sub'), parts along dimension 0, may hold values from -6 to 6
- y_start: float32 [16384, 256], P(('lp', 'col', 'row'), 'sub'), parts along dimension 0, may hold values from 0 to 1
- demand: float32 [16384, 16], P(('lp', 'col', 'row')), parts along dimension 0, may hold values from 0.2 to 24, as said below
- scen_level: int32 [512], P(('lp', 'sub')), parts along dimension 0, may hold values from 0 to 15
- cost: float32 [2048], P(('lp', 'col', 'row')), parts along dimension 0, may hold values from 0.2 to 18, as said below
- upper: float32 [2048], P(('lp', 'col', 'row')), parts along dimension 0, may hold values from 0.2 to 2
- bound_type: int32 [2048], P(('lp', 'col', 'row')), parts along dimension 0, may hold values from 0 to 2
Outputs:
- primal_out: float32 [2048, 256], P(('lp', 'col', 'row'), 'sub'), parts along dimension 0
- dual_out: float32 [16384, 256], P(('lp', 'col', 'row'), 'sub'), parts along dimension 0
- ray_scores: float32 [4, 512], P(None, ('lp', 'sub')), parts along dimension 1
There are 2 independent parts, one for each index of `lp`. A program takes and returns all parts, laid end to end along the dimension named above; each array names one. Nothing has to cross between parts.
Inputs may be any that keep to these rules, and one draw needn't show every extreme that they name: `band_cols`: row block i belongs to col group c = i // 16; each of its tiles lies in a column block of col group c - 1, c or c + 1 taken cyclically, group g holding column blocks g * 2 to (g + 1) * 2 - 1. Tile 0 of row block i is column block c * 2 + (i mod 2). `demand`: positive. `cost`: positive. `bound_type`: 0: lower bound 0 only; 1: between 0 and upper; 2: free.
All inputs are finite; a program needn't handle non-finite values.
Results may differ from a plain program's by a relative error of at most 0.00092.
Values may be sent and summed in bfloat16 or wider, within the bound.
A program may use at most 64 MiB of HBM per device.

v0:
```python
import jax
import jax.numpy as jnp
from jax import lax
from jax.sharding import PartitionSpec as P

ITERS = 2


step_primal = 0.3
step_dual = 0.3
eps = 1e-06


def from_behind(value, axis, by):
    count = lax.axis_size(axis)
    return lax.ppermute(value, axis, [(i, (i + by) % count) for i in range(count)])


def clamp_box(value, upper, bound_type):
    lower_only = jnp.maximum(value, 0.0)
    boxed = jnp.minimum(lower_only, upper[:, None])
    return jnp.where(
        bound_type[:, None] == 0, lower_only, jnp.where(bound_type[:, None] == 1, boxed, value)
    )


def on_device(matrix, band_cols, x_start, y_start, demand, scen_level, cost, upper, bound_type):
    row_blocks, band_size, block_size, _ = matrix.shape
    panel_width = x_start.shape[1]
    col_blocks = x_start.shape[0] // block_size
    col_count = lax.axis_size("col")
    row_count = lax.axis_size("row")
    group_size = row_count * col_blocks
    col_index = lax.axis_index("col")
    offset = (band_cols // group_size - col_index + col_count) % col_count
    slab_id = jnp.where(offset == 0, 1, jnp.where(offset == 1, 2, 0))
    tile_cols = (slab_id * group_size + band_cols % group_size).reshape(-1)
    level_table = (
        jnp.arange(demand.shape[1], dtype=jnp.int32)[:, None] == scen_level[None, :]
    ).astype(jnp.float32)
    demand_panel = jnp.dot(demand, level_table, precision=lax.Precision.HIGHEST)
    primal = x_start
    dual = y_start
    collected = []
    for step in range(ITERS):
        products = jnp.einsum(
            "ikab,ias->ikbs",
            matrix,
            dual.astype(jnp.bfloat16).reshape(row_blocks, block_size, panel_width),
            preferred_element_type=jnp.float32,
        )
        partial_value = jax.ops.segment_sum(
            products.reshape(row_blocks * band_size, block_size, panel_width),
            tile_cols,
            num_segments=3 * group_size,
        )
        partial_value = partial_value.reshape(3, group_size * block_size, panel_width)
        summed = partial_value[1]
        for backward_step_by, slab_pick in ((-1, 0), (1, 2)):
            summed = summed + from_behind(partial_value[slab_pick], "col", backward_step_by)
        pull_back = lax.psum_scatter(summed, "row", scatter_dimension=0, tiled=True)
        primal_next = clamp_box(
            primal - step_primal * (cost[:, None] - pull_back), upper, bound_type
        )
        extrapolated = (2.0 * primal_next - primal).astype(jnp.bfloat16)
        entire = lax.all_gather(extrapolated, "row", axis=0, tiled=True)
        beside = [from_behind(entire, "col", step_by) for step_by in (1, -1)]
        stacked = jnp.stack([beside[0], entire, beside[1]])
        gathered = jnp.take(
            stacked.reshape(3 * group_size, block_size, panel_width), tile_cols, axis=0
        )
        gathered = gathered.reshape(row_blocks, band_size, block_size, panel_width)
        result = jnp.einsum("ikab,ikbs->ias", matrix, gathered, preferred_element_type=jnp.float32)
        push_forward = result.reshape(row_blocks * block_size, panel_width)
        dual_next = jnp.maximum(dual + step_dual * (demand_panel - push_forward), 0.0)
        primal_step = primal_next - primal
        dual_step = dual_next - dual
        partial_sums = jnp.stack(
            [
                -jnp.sum(cost[:, None] * primal_step, axis=0),
                jnp.sum(primal_step * primal_step, axis=0),
                jnp.sum(demand_panel * dual_step, axis=0),
                jnp.sum(dual_step * dual_step, axis=0),
            ]
        )
        collected.append(lax.psum(partial_sums, ("col", "row")))
        primal = primal_next
        dual = dual_next
    stacked_sums = jnp.stack(collected)
    total_cols = float(col_count * row_count * col_blocks * block_size)
    total_rows = float(col_count * row_count * row_blocks * block_size)
    primal_score = stacked_sums[:, 0] / (
        total_cols * jnp.sqrt(stacked_sums[:, 1] / total_cols + eps)
    )
    dual_score = stacked_sums[:, 2] / (total_rows * jnp.sqrt(stacked_sums[:, 3] / total_rows + eps))
    ray_scores = jnp.stack([primal_score, dual_score], axis=1).reshape(2 * ITERS, panel_width)
    return (primal, dual, ray_scores)


def solution(mesh):
    placed = (
        P(("lp", "col", "row"), None, None, None),
        P(("lp", "col", "row"), None),
        P(("lp", "col", "row"), "sub"),
        P(("lp", "col", "row"), "sub"),
        P(("lp", "col", "row"), None),
        P(("lp", "sub")),
        P(("lp", "col", "row")),
        P(("lp", "col", "row")),
        P(("lp", "col", "row")),
    )
    return jax.shard_map(
        on_device,
        mesh=mesh,
        in_specs=placed,
        out_specs=(
            P(("lp", "col", "row"), "sub"),
            P(("lp", "col", "row"), "sub"),
            P(None, ("lp", "sub")),
        ),
        check_vma=False,
    )
```

profile of v0, /device:TPU:0, one launch (start us, length us, event | category | flops | bytes accessed | tf_op | source)
XLA Modules:
  0.0 161.0 jit_solution(16473907660012646569)
XLA Ops:
  9.3 3.3 %fusion.20 = f32[8,10,128,128]{3,2,1,0:T(8,128)} fusion(bf16[8,10,128,128]{3,2,1,0:T(8,128)(2,1)S(1)} %copy-done, bf16[8,128,128,1]{2,1,3,0:T(8,128)(2,1)S(1)} %bitcast.83), kind=kOutput, calls=%fused_computation.70 | convolution fusion | flops 335544320 | bytes 8126464 | tf_op jit(solution)/shard_map/ikab,ias->ikbs/dot_general | solution.py:46
  12.6 10.8 %scatter_fusion = f32[6,128,128]{2,1,0:T(8,128)S(1)} fusion(f32[6,128,128]{2,1,0:T(8,128)S(1)} %broadcast.72.clone, s32[80]{0:T(128)S(1)} %reshape.114, f32[80,128,128]{2,1,0:T(8,128)} %bitcast.77), kind=kCustom, calls=%fused_computation.2 | custom fusion | flops 1310720 | bytes 15728960 | tf_op jit(solution)/shard_map/scatter-add | solution.py:52
  23.5 5.1 %collective-permute-start = (f32[256,128]{1,0:T(8,128)S(1)}, f32[256,128]{1,0:T(8,128)S(1)}, u32[]{:S(2)}, u32[]{:S(2)}) collective-permute-start(f32[256,128]{1,0:T(8,128)S(1)} %bitcast.88), channel_id=1, source_target_pairs={{0,12},{4,0},{8,4},{12,8},{1,13},{5,1},{9,5},{13,9},{2,14},{6,2},{... | collective-permute-start | bytes 393224 | tf_op jit(solution)/shard_map/ppermute | solution.py:16
  28.6 3.9 %collective-permute-done = f32[256,128]{1,0:T(8,128)S(1)} collective-permute-done((f32[256,128]{1,0:T(8,128)S(1)}, f32[256,128]{1,0:T(8,128)S(1)}, u32[]{:S(2)}, u32[]{:S(2)}) %collective-permute-start) | collective-permute-done | bytes 131104 | tf_op jit(solution)/shard_map/ppermute | solution.py:16
  32.5 2.9 %collective-permute-done.1 = f32[256,128]{1,0:T(8,128)S(1)} collective-permute-done((f32[256,128]{1,0:T(8,128)S(1)}, f32[256,128]{1,0:T(8,128)S(1)}, u32[]{:S(2)}, u32[]{:S(2)}) %collective-permute-start.1) | collective-permute-done | bytes 131104 | tf_op jit(solution)/shard_map/ppermute | solution.py:16
  37.8 2.1 %convolution_bitcast_fusion = f32[1024,128]{0,1:T(8,128)} fusion(f32[1024,16]{0,1:T(8,128)} %param.15, s32[128]{0:T(128)} %param.16), kind=kOutput, calls=%fused_computation.6 | convolution fusion | flops 25167872 | bytes 590336 | tf_op jit(solution)/shard_map/dot_general | solution.py:41
  39.9 5.6 %reduce-scatter.3.cloned.1.call-done = f32[128,128]{1,0:T(8,128)} async-done(((f32[256,128]{1,0:T(8,128)}), f32[128,128]{1,0:T(8,128)}) %reduce-scatter.3.cloned.1.call-update) | async-done | bytes 65552 | tf_op jit(solution)/shard_map/reduce_scatter | solution.py:61
  47.2 4.6 %all_gather.6 = bf16[256,128]{1,0:T(8,128)(2,1)S(1)} all-gather(bf16[128,128]{1,0:T(8,128)(2,1)S(1)} %get-tuple-element.26), channel_id=1, replica_groups=mesh['lp'=2,'col'=4,'row'=2,'sub'=2] {'row'}, dimensions={0}, use_global_device_ids=true | all-gather | bytes 98304 | tf_op jit(solution)/shard_map/all_gather | solution.py:66
  51.7 3.3 %collective-permute-start.3 = (bf16[256,128]{1,0:T(8,128)(2,1)S(1)}, bf16[256,128]{1,0:T(8,128)(2,1)S(1)}, u32[]{:S(2)}, u32[]{:S(2)}) collective-permute-start(bf16[256,128]{1,0:T(8,128)(2,1)S(1)} %all_gather.6), channel_id=1, source_target_pairs={{0,12},{4,0},{8,4},{12,8},{1,13},{5,1},{9,5},{13,9},{2,14},{6,2},{... | collective-permute-start | bytes 196616 | tf_op jit(solution)/shard_map/ppermute | solution.py:16
  57.0 4.2 %collective-permute-done.2 = bf16[256,128]{1,0:T(8,128)(2,1)S(1)} collective-permute-done((bf16[256,128]{1,0:T(8,128)(2,1)S(1)}, bf16[256,128]{1,0:T(8,128)(2,1)S(1)}, u32[]{:S(2)}, u32[]{:S(2)}) %collective-permute-start.2) | collective-permute-done | bytes 65568 | tf_op jit(solution)/shard_map/ppermute | solution.py:16
  61.2 2.5 %gather_fusion = bf16[80,128,128]{2,1,0:T(8,128)(2,1)} fusion(bf16[6,128,128]{2,1,0:T(8,128)(2,1)S(1)} %bitcast.76, s32[1024]{0:T(1024)S(1)} %pad_clamp_fusion), kind=kCustom, calls=%fused_computation.clone | custom fusion | bytes 5243200 | tf_op jit(solution)/shard_map/jit(_take)/gather | solution.py:69
  67.4 2.1 %copy.32 = f32[1024,128]{0,1:T(8,128)} copy(f32[1024,128]{1,0:T(8,128)} %bitcast.81) | data formatting | bytes 1048576 | tf_op jit(solution)/shard_map/reshape | solution.py:74
  69.5 2.2 %convert_bitcast_fusion = (bf16[16,8,8,128]{3,1,2,0:T(8,128)(2,1)S(1)}, f32[1024,128]{0,1:T(8,128)}) fusion(f32[1024,128]{0,1:T(8,128)S(1)} %copy.21, f32[1024,128]{0,1:T(8,128)} %convolution_bitcast_fusion, f32[1024,128]{0,1:T(8,128)} %copy.32), kind=kLoop, calls=%fused_computation.15 | loop fusion | flops 655360 | bytes 2359296
  71.7 3.1 %fusion = f32[8,128,10,128]{3,1,2,0:T(8,128)} fusion(bf16[8,10,128,128]{3,2,1,0:T(8,128)(2,1)S(1)} %copy-done, bf16[8,128,128,1]{1,0,2,3:T(8,128)(2,1)S(1)} %bitcast.84), kind=kOutput, calls=%fused_computation.13 | convolution fusion | flops 335544320 | bytes 8126464 | tf_op jit(solution)/shard_map/ikab,ias->ikbs/dot_general | solution.py:46
  74.8 6.0 %copy.23 = f32[80,128,128]{2,1,0:T(8,128)} copy(f32[80,128,128]{1,2,0:T(8,128)} %bitcast.78) | data formatting | bytes 10485760 | tf_op jit(solution)/shard_map/reshape | solution.py:53
  80.8 10.8 %scatter_fusion.1 = f32[6,128,128]{2,1,0:T(8,128)S(1)} fusion(f32[6,128,128]{2,1,0:T(8,128)S(1)} %broadcast.72, s32[80]{0:T(128)S(1)} %reshape.114, f32[80,128,128]{2,1,0:T(8,128)} %copy.23), kind=kCustom, calls=%fused_computation.3 | custom fusion | flops 1310720 | bytes 15728960 | tf_op jit(solution)/shard_map/scatter-add | solution.py:52
  93.8 3.4 %collective-permute-done.4 = f32[256,128]{1,0:T(8,128)S(1)} collective-permute-done((f32[256,128]{1,0:T(8,128)S(1)}, f32[256,128]{1,0:T(8,128)S(1)}, u32[]{:S(2)}, u32[]{:S(2)}) %collective-permute-start.4) | collective-permute-done | bytes 131104 | tf_op jit(solution)/shard_map/ppermute | solution.py:16
  99.3 7.7 %reduce-scatter.5.cloned.1.call-done = f32[128,128]{1,0:T(8,128)} async-done(((f32[256,128]{1,0:T(8,128)}), f32[128,128]{1,0:T(8,128)}) %reduce-scatter.5.cloned.1.call-update) | async-done | bytes 65552 | tf_op jit(solution)/shard_map/reduce_scatter | solution.py:61
  109.4 4.6 %all_gather.7 = bf16[256,128]{1,0:T(8,128)(2,1)S(1)} all-gather(bf16[128,128]{1,0:T(8,128)(2,1)S(1)} %subtract_convert_fusion), channel_id=1, replica_groups=mesh['lp'=2,'col'=4,'row'=2,'sub'=2] {'row'}, dimensions={0}, use_global_device_ids=true | all-gather | bytes 98304 | tf_op jit(solution)/shard_map/all_gather | solution.py:66
  115.5 2.4 %collective-permute-start.7 = (bf16[256,128]{1,0:T(8,128)(2,1)S(1)}, bf16[256,128]{1,0:T(8,128)(2,1)S(1)}, u32[]{:S(2)}, u32[]{:S(2)}) collective-permute-start(bf16[256,128]{1,0:T(8,128)(2,1)S(1)} %all_gather.7), channel_id=1, source_target_pairs={{0,12},{4,0},{8,4},{12,8},{1,13},{5,1},{9,5},{13,9},{2,14},{6,2},{... | collective-permute-start | bytes 196616 | tf_op jit(solution)/shard_map/ppermute | solution.py:16
  117.9 2.3 %collective-permute-done.6 = bf16[256,128]{1,0:T(8,128)(2,1)S(1)} collective-permute-done((bf16[256,128]{1,0:T(8,128)(2,1)S(1)}, bf16[256,128]{1,0:T(8,128)(2,1)S(1)}, u32[]{:S(2)}, u32[]{:S(2)}) %collective-permute-start.6) | collective-permute-done | bytes 65568 | tf_op jit(solution)/shard_map/ppermute | solution.py:16
  120.5 2.5 %gather_fusion.1 = bf16[80,128,128]{2,1,0:T(8,128)(2,1)} fusion(bf16[6,128,128]{2,1,0:T(8,128)(2,1)S(1)} %bitcast.75, s32[1024]{0:T(1024)S(1)} %pad_clamp_fusion), kind=kCustom, calls=%fused_computation.1.clone | custom fusion | bytes 5243200 | tf_op jit(solution)/shard_map/jit(_take)/gather | solution.py:69
  128.8 2.4 %multiply_reduce_fusion.1 = (f32[128]{0:T(128)S(1)}, f32[128]{0:T(128)S(1)}, f32[128]{0:T(128)S(1)}, f32[128]{0:T(128)S(1)}, f32[1024,128]{0,1:T(8,128)}) fusion(f32[1024,128]{0,1:T(8,128)} %convolution_bitcast_fusion, f32[1024,128]{0,1:T(8,128)} %get-tuple-element.25, f32[1024,128]{0,1:T(8,128)S(1)} %copy.21, f32[1024,128]{0,1:T(8,128)} %copy.35), kind=kLoop, calls=%fused_computation.8 | loop fusion | flops 1834496 | bytes 2623488 | tf_op jit(solution)/shard_map/reduce_sum | solution.py:82
  131.2 20.3 %all-reduce = (f32[1,4,128]{2,1,0:T(4,128)S(1)}, f32[1,4,128]{2,1,0:T(4,128)S(1)}) all-reduce(f32[1,4,128]{2,1,0:T(4,128)S(1)} %maximum_bitcast_fusion, f32[1,4,128]{2,1,0:T(4,128)S(1)} %maximum_bitcast_fusion.1), channel_id=1, replica_groups=mesh['lp'=2,'col'=4,'row'=2,'sub'=2] {'col','row'}, use_global_device_ids=true, to_apply=%region_8.10 | all-reduce | flops 1024 | bytes 8192 | tf_op jit(solution)/shard_map/psum | solution.py:86
  (67 shorter events, 28.8 us)
Async XLA Ops:
  7.2 2.1 %copy-start = (bf16[8,10,128,128]{3,2,1,0:T(8,128)(2,1)S(1)}, bf16[8,10,128,128]{3,2,1,0:T(8,128)(2,1)}, u32[]{:S(2)}) copy-start(bf16[8,10,128,128]{3,2,1,0:T(8,128)(2,1)} %param.11) | copy-start | bytes 7864324
  7.2 38.3 %reduce-scatter.3.cloned.1.call-start = ((), (), s32[]{:S(2)}) async-start(), calls=%async_computation.2 | async-start | bytes 196608 | tf_op jit(solution)/shard_map/reduce_scatter | solution.py:61
  12.5 16.0 %copy-start.10 = (s32[128]{0:T(128)S(1)}, s32[128]{0:T(128)}, u32[]{:S(2)}) copy-start(s32[128]{0:T(128)} %param.19) | copy-start | bytes 1540
  23.4 22.1 %copy-start.2 = (f32[128]{0:T(128)S(1)}, f32[128]{0:T(128)}, u32[]{:S(2)}) copy-start(f32[128]{0:T(128)} %param.17) | copy-start | bytes 1540
  23.4 22.1 %copy-start.3 = (f32[128]{0:T(128)S(1)}, f32[128]{0:T(128)}, u32[]{:S(2)}) copy-start(f32[128]{0:T(128)} %param.18) | copy-start | bytes 1540
  23.5 9.0 %collective-permute-start = (f32[256,128]{1,0:T(8,128)S(1)}, f32[256,128]{1,0:T(8,128)S(1)}, u32[]{:S(2)}, u32[]{:S(2)}) collective-permute-start(f32[256,128]{1,0:T(8,128)S(1)} %bitcast.88), channel_id=1, source_target_pairs={{0,12},{4,0},{8,4},{12,8},{1,13},{5,1},{9,5},{13,9},{2,14},{6,2},{... | collective-permute-start | bytes 393224 | tf_op jit(solution)/shard_map/ppermute | solution.py:16
  28.6 6.8 %collective-permute-start.1 = (f32[256,128]{1,0:T(8,128)S(1)}, f32[256,128]{1,0:T(8,128)S(1)}, u32[]{:S(2)}, u32[]{:S(2)}) collective-permute-start(f32[256,128]{1,0:T(8,128)S(1)} %bitcast.87), channel_id=1, source_target_pairs={{0,4},{4,8},{8,12},{12,0},{1,5},{5,9},{9,13},{13,1},{2,6},{6,10},{... | collective-permute-start | bytes 393224 | tf_op jit(solution)/shard_map/ppermute | solution.py:16
  28.6 18.6 %copy-start.5 = (pred[128]{0:T(512)(128)(4,1)}, pred[128]{0:T(512)(128)(4,1)S(1)}, u32[]{:S(2)}) copy-start(pred[128]{0:T(512)(128)(4,1)S(1)} %get-tuple-element.37) | copy-start | bytes 388
  28.6 26.5 %copy-start.4 = (pred[128]{0:T(512)(128)(4,1)}, pred[128]{0:T(512)(128)(4,1)S(1)}, u32[]{:S(2)}) copy-start(pred[128]{0:T(512)(128)(4,1)S(1)} %get-tuple-element.36) | copy-start | bytes 388
  36.0 70.9 %reduce-scatter.5.cloned.1.call-start = ((), (), s32[]{:S(2)}) async-start(), calls=%async_computation.3 | async-start | bytes 196608 | tf_op jit(solution)/shard_map/reduce_scatter | solution.py:61
  51.7 5.2 %collective-permute-start.3 = (bf16[256,128]{1,0:T(8,128)(2,1)S(1)}, bf16[256,128]{1,0:T(8,128)(2,1)S(1)}, u32[]{:S(2)}, u32[]{:S(2)}) collective-permute-start(bf16[256,128]{1,0:T(8,128)(2,1)S(1)} %all_gather.6), channel_id=1, source_target_pairs={{0,12},{4,0},{8,4},{12,8},{1,13},{5,1},{9,5},{13,9},{2,14},{6,2},{... | collective-permute-start | bytes 196616 | tf_op jit(solution)/shard_map/ppermute | solution.py:16
  55.1 6.1 %collective-permute-start.2 = (bf16[256,128]{1,0:T(8,128)(2,1)S(1)}, bf16[256,128]{1,0:T(8,128)(2,1)S(1)}, u32[]{:S(2)}, u32[]{:S(2)}) collective-permute-start(bf16[256,128]{1,0:T(8,128)(2,1)S(1)} %all_gather.6), channel_id=1, source_target_pairs={{0,4},{4,8},{8,12},{12,0},{1,5},{5,9},{9,13},{13,1},{2,6},{6,10},{... | collective-permute-start | bytes 196616 | tf_op jit(solution)/shard_map/ppermute | solution.py:16
  61.2 2.6 %copy-start.8 = (pred[80]{0:T(512)(128)(4,1)S(1)}, pred[80]{0:T(512)(128)(4,1)}, u32[]{:S(2)}) copy-start(pred[80]{0:T(512)(128)(4,1)} %compare_and_fusion) | copy-start | bytes 244
  91.7 5.5 %collective-permute-start.4 = (f32[256,128]{1,0:T(8,128)S(1)}, f32[256,128]{1,0:T(8,128)S(1)}, u32[]{:S(2)}, u32[]{:S(2)}) collective-permute-start(f32[256,128]{1,0:T(8,128)S(1)} %bitcast.90), channel_id=1, source_target_pairs={{0,12},{4,0},{8,4},{12,8},{1,13},{5,1},{9,5},{13,9},{2,14},{6,2},{... | collective-permute-start | bytes 393224 | tf_op jit(solution)/shard_map/ppermute | solution.py:16
  91.8 6.8 %collective-permute-start.5 = (f32[256,128]{1,0:T(8,128)S(1)}, f32[256,128]{1,0:T(8,128)S(1)}, u32[]{:S(2)}, u32[]{:S(2)}) collective-permute-start(f32[256,128]{1,0:T(8,128)S(1)} %bitcast.89), channel_id=1, source_target_pairs={{0,4},{4,8},{8,12},{12,0},{1,5},{5,9},{9,13},{13,1},{2,6},{6,10},{... | collective-permute-start | bytes 393224 | tf_op jit(solution)/shard_map/ppermute | solution.py:16
  108.6 14.5 %copy-start.1 = (f32[128,128]{1,0:T(8,128)}, f32[128,128]{1,0:T(8,128)S(1)}, u32[]{:S(2)}) copy-start(f32[128,128]{1,0:T(8,128)S(1)} %get-tuple-element.22) | copy-start | bytes 196612
  114.0 6.2 %collective-permute-start.6 = (bf16[256,128]{1,0:T(8,128)(2,1)S(1)}, bf16[256,128]{1,0:T(8,128)(2,1)S(1)}, u32[]{:S(2)}, u32[]{:S(2)}) collective-permute-start(bf16[256,128]{1,0:T(8,128)(2,1)S(1)} %all_gather.7), channel_id=1, source_target_pairs={{0,4},{4,8},{8,12},{12,0},{1,5},{5,9},{9,13},{13,1},{2,6},{6,10},{... | collective-permute-start | bytes 196616 | tf_op jit(solution)/shard_map/ppermute | solution.py:16
  115.5 5.0 %collective-permute-start.7 = (bf16[256,128]{1,0:T(8,128)(2,1)S(1)}, bf16[256,128]{1,0:T(8,128)(2,1)S(1)}, u32[]{:S(2)}, u32[]{:S(2)}) collective-permute-start(bf16[256,128]{1,0:T(8,128)(2,1)S(1)} %all_gather.7), channel_id=1, source_target_pairs={{0,12},{4,0},{8,4},{12,8},{1,13},{5,1},{9,5},{13,9},{2,14},{6,2},{... | collective-permute-start | bytes 196616 | tf_op jit(solution)/shard_map/ppermute | solution.py:16
  120.5 2.6 %copy-start.9 = (pred[80]{0:T(512)(128)(4,1)S(1)}, pred[80]{0:T(512)(128)(4,1)}, u32[]{:S(2)}) copy-start(pred[80]{0:T(512)(128)(4,1)} %compare_and_fusion) | copy-start | bytes 244
  126.7 4.5 %copy-start.7 = (f32[128]{0:T(128)S(1)}, f32[128]{0:T(128)}, u32[]{:S(2)}) copy-start(f32[128]{0:T(128)} %get-tuple-element.15) | copy-start | bytes 1540
  126.7 4.5 %copy-start.6 = (f32[128]{0:T(128)S(1)}, f32[128]{0:T(128)}, u32[]{:S(2)}) copy-start(f32[128]{0:T(128)} %get-tuple-element.18) | copy-start | bytes 1540
Sparse Core Ops, SparseCore 0:
  36.1 9.3 reduce-scatter.2
  99.4 7.4 reduce-scatter.4
where the time goes:
time: 162 us; the launch traced here: 161 us
  other arithmetic  38.9 us (24%)
  waiting for transfers between devices  33.5 us (21%)
  blocking collectives  29.4 us (18%)
  local copies, waits for them, and re-layouts  18.7 us (12%)
  starting transfers between devices  14.4 us (9%)
  between operations  14.3 us (9%)
  matrix products  11.7 us (7%)
    scatter-add x2, other arithmetic, on_device(): jax.ops.segment_sum(products.reshape(row_blocks * band_size, block_size,...  21.7 us
    psum x1, blocking collectives, on_device(): collected.append(lax.psum(partial_sums, ('col', 'row')))  20.3 us
    ppermute x8, waiting for transfers between devices, from_behind(): lax.ppermute(value, axis, [(i, (i + by) % count) for i in range(count)])  20.2 us
    ppermute x8, starting transfers between devices, from_behind(): lax.ppermute(value, axis, [(i, (i + by) % count) for i in range(count)])  14.3 us
    reduce_scatter x2, waiting for transfers between devices, on_device(): pull_back = lax.psum_scatter(summed, 'row', scatter_dimension=0, tiled=True)  13.3 us
    all_gather x2, blocking collectives, on_device(): entire = lax.all_gather(extrapolated, 'row', axis=0, tiled=True)  9.17 us
    dot_general x2, matrix products, on_device(): jnp.einsum('ikab,ias->ikbs', matrix, dual.astype(jnp.bfloat16).reshape(ro...  6.41 us
    reshape x1, local copies, waits for them, and re-layouts, on_device(): products.reshape(row_blocks * band_size, block_size, panel_width)  5.96 us
  transfers between devices with their start and end apart: 10, of which 10 were waited for; matrix products, arithmetic and copies ran while one was open for 2% of the time, Pallas kernels for 0%

commit v1 on v0

v1 whole, which is shorter than its diff:
```python
import functools

import jax
import jax.numpy as jnp
from jax import lax
from jax.experimental import pallas as pl
from jax.experimental.pallas import tpu as pltpu
from jax.sharding import PartitionSpec as P

ITERS = 2
step_primal = 0.3
step_dual = 0.3
eps = 1e-06
MESH = pl.DeviceIdType.MESH
CHUNK = 32


def dot(a, b):
    return jnp.dot(a, b, preferred_element_type=jnp.float32)


def kernel(C, R, cols_ref, mat_hbm, x_hbm, y_hbm, dem_ref, level_ref, cost_ref, upper_ref, kind_ref,
           x_out, y_out, score_ref,
           mat, hi, lo, xv, yv, panel, dual_t, pbuf, rbuf, xbuf, sums, others,
           mat_sem, in_sem, out_sem, p_send, p_recv, x_send, x_recv, s_send, s_recv):
    row_blocks, band, blk, _ = mat.shape
    rows = row_blocks * blk
    levels = dem_ref.shape[0]
    ci, ri = lax.axis_index("col"), lax.axis_index("row")

    def peer(dc, dr):
        return {"col": lax.rem(ci + dc + C, C), "row": lax.rem(ri + dr, R)}

    peers = [(dc, dr) for dc in range(C) for dr in range(R) if (dc, dr) != (0, 0)]

    y_in = pltpu.make_async_copy(y_hbm, yv, in_sem.at[0])
    x_in = pltpu.make_async_copy(x_hbm, xv, in_sem.at[1])

    def mat_in(i):
        return pltpu.make_async_copy(mat_hbm.at[i], mat.at[i], mat_sem.at[i])

    mat_in(0).start()
    y_in.start()
    x_in.start()
    for i in range(1, row_blocks):
        mat_in(i).start()

    barrier = pltpu.get_barrier_semaphore()
    for dc, dr in peers:
        pl.semaphore_signal(barrier, inc=1, device_id=peer(dc, dr), device_id_type=MESH)

    slot_col = [lax.rem(ci + s - 1 + C, C) * R + w for s in range(3) for w in range(R)]

    def densify(i, carry):
        mat_in(i).wait()
        marks = []
        for k in range(band):
            col = cols_ref[i, k]
            marks.append([jnp.where(col == c, 1.0, 0.0).astype(jnp.float32) for c in slot_col])

        def part(r, carry):
            at = pl.ds(pl.multiple_of(r * CHUNK, CHUNK), CHUNK)
            to = pl.ds(pl.multiple_of(i * blk + r * CHUNK, CHUNK), CHUNK)
            total = [None] * (3 * R)
            for k in range(band):
                tile = mat[i, k, at, :].astype(jnp.float32)
                for j in range(3 * R):
                    term = marks[k][j] * tile
                    total[j] = term if k == 0 else total[j] + term
            for j in range(3 * R):
                s, w = j // R, j % R
                top = total[j].astype(jnp.bfloat16)
                hi[s, to, w * blk:(w + 1) * blk] = top
                lo[s, to, w * blk:(w + 1) * blk] = (total[j] - top.astype(jnp.float32)).astype(jnp.bfloat16)
            return carry

        return lax.fori_loop(0, blk // CHUNK, part, carry)

    lax.fori_loop(0, row_blocks, densify, 0)

    y_in.wait()
    for i in range(row_blocks):
        dual_t[:, i * blk:(i + 1) * blk] = yv[i * blk:(i + 1) * blk, :].T.astype(jnp.bfloat16)
    pl.semaphore_wait(barrier, len(peers))

    def down(t, s, dr):
        w = lax.rem(ri + dr, R)
        return pltpu.make_async_remote_copy(
            src_ref=pbuf.at[t, s, w], dst_ref=rbuf.at[t, s, dr],
            send_sem=p_send.at[t, s, dr], recv_sem=p_recv.at[t, s, dr],
            device_id=peer(s - 1, dr), device_id_type=MESH)

    def up(t, s, dr):
        return pltpu.make_async_remote_copy(
            src_ref=xbuf.at[t, 1, ri], dst_ref=xbuf.at[t, s, ri],
            send_sem=x_send.at[t, s, dr], recv_sem=x_recv.at[t, s, dr],
            device_id=peer(1 - s, dr), device_id_type=MESH)

    def arrival(t, s, dr):
        w = lax.rem(ri - dr + R, R)
        return pltpu.make_async_remote_copy(
            src_ref=xbuf.at[t, 1, ri], dst_ref=xbuf.at[t, s, w],
            send_sem=x_send.at[t, s, dr], recv_sem=x_recv.at[t, s, dr],
            device_id=peer(1 - s, dr), device_id_type=MESH)

    moves = [(s, dr) for s in (0, 2, 1) for dr in range(R) if (s, dr) != (1, 0)]

    for t in range(ITERS):
        d = dual_t[...]
        for s in (0, 2, 1):
            product = dot(d, hi[s]) + dot(d, lo[s])
            for w in range(R):
                pbuf[t, s, w] = product[:, w * blk:(w + 1) * blk]
            for dr in range(R):
                if (s, dr) != (1, 0):
                    down(t, s, dr).start()
        if t == 0:
            x_in.wait()
            rows_of = lax.broadcasted_iota(jnp.int32, (levels, blk), 0)
            pick = jnp.where(rows_of == level_ref[...], 1.0, 0.0).astype(jnp.bfloat16)
            part_1 = dem_ref[...].astype(jnp.bfloat16)
            rest = dem_ref[...] - part_1.astype(jnp.float32)
            part_2 = rest.astype(jnp.bfloat16)
            part_3 = (rest - part_2.astype(jnp.float32)).astype(jnp.bfloat16)
            along = (((0,), (0,)), ((), ()))
            parts = [lax.dot_general(q, pick, along, preferred_element_type=jnp.float32)
                     for q in (part_1, part_2, part_3)]
            panel[...] = parts[0] + (parts[1] + parts[2])
            cost = jnp.broadcast_to(cost_ref[...], (blk, blk)).T
            upper = jnp.broadcast_to(upper_ref[...], (blk, blk)).T
            kind = jnp.broadcast_to(kind_ref[...], (blk, blk)).astype(jnp.float32).T
        pulled = pbuf[t, 1, ri]
        for s, dr in moves[::-1]:
            down(t, s, dr).wait_recv()
            pulled = pulled + rbuf[t, s, dr]
        primal = xv[...]
        value = primal - step_primal * (cost - pulled.T)
        low = jnp.maximum(value, 0.0)
        primal_next = jnp.where(kind == 0.0, low, jnp.where(kind == 1.0, jnp.minimum(low, upper), value))
        xbuf[t, 1, ri] = (2.0 * primal_next - primal).astype(jnp.bfloat16)
        for s, dr in moves:
            up(t, s, dr).start()
        primal_step = primal_next - primal
        xv[...] = primal_next
        if t == ITERS - 1:
            x_done = pltpu.make_async_copy(xv, x_out, out_sem.at[row_blocks])
            x_done.start()
        sums[4 * t:4 * t + 1, :] = -jnp.sum(cost * primal_step, axis=0, keepdims=True)
        sums[4 * t + 1:4 * t + 2, :] = jnp.sum(primal_step * primal_step, axis=0, keepdims=True)

        accs = [None] * row_blocks
        for s in (1, 0, 2):
            for dr in range(R):
                if (s, dr) != (1, 0):
                    arrival(t, s, dr).wait_recv()
            x = xbuf[t, s].reshape(R * blk, blk)
            for i in range(row_blocks):
                at = slice(i * blk, (i + 1) * blk)
                term = dot(hi[s, at, :], x) + dot(lo[s, at, :], x)
                accs[i] = term if accs[i] is None else accs[i] + term
        along_rows = jnp.zeros((8, blk), jnp.float32)
        squares = jnp.zeros((8, blk), jnp.float32)
        y_done = []
        for i in range(row_blocks):
            at = slice(i * blk, (i + 1) * blk)
            dual = yv[at, :]
            want = panel[at, :]
            dual_next = jnp.maximum(dual + step_dual * (want - accs[i]), 0.0)
            yv[at, :] = dual_next
            if t == ITERS - 1:
                y_done.append(pltpu.make_async_copy(yv.at[at, :], y_out.at[at, :], out_sem.at[i]))
                y_done[-1].start()
            else:
                dual_t[:, at] = dual_next.T.astype(jnp.bfloat16)
            dual_step = dual_next - dual
            along_rows += jnp.sum((want * dual_step).reshape(-1, 8, blk), axis=0)
            squares += jnp.sum((dual_step * dual_step).reshape(-1, 8, blk), axis=0)
        sums[4 * t + 2:4 * t + 3, :] = jnp.sum(along_rows, axis=0, keepdims=True)
        sums[4 * t + 3:4 * t + 4, :] = jnp.sum(squares, axis=0, keepdims=True)

    def share(n):
        return pltpu.make_async_remote_copy(
            src_ref=sums, dst_ref=others.at[n], send_sem=s_send.at[n], recv_sem=s_recv.at[n],
            device_id=peer(*peers[n]), device_id_type=MESH)

    for n in range(len(peers)):
        share(n).start()
    total = sums[...]
    for n in range(len(peers)):
        share(n).wait_recv()
        total = total + others[n]
    col_total = float(C * R * blk)
    row_total = float(C * R * rows)
    for t in range(ITERS):
        score_ref[2 * t:2 * t + 1, :] = total[4 * t:4 * t + 1, :] / (
            col_total * jnp.sqrt(total[4 * t + 1:4 * t + 2, :] / col_total + eps))
        score_ref[2 * t + 1:2 * t + 2, :] = total[4 * t + 2:4 * t + 3, :] / (
            row_total * jnp.sqrt(total[4 * t + 3:4 * t + 4, :] / row_total + eps))
    for t in range(ITERS):
        for s, dr in moves:
            down(t, s, dr).wait_send()
            up(t, s, dr).wait_send()
    for n in range(len(peers)):
        share(n).wait_send()
    x_done.wait()
    for copy in y_done:
        copy.wait()


def solution(mesh):
    C, R = mesh.shape["col"], mesh.shape["row"]

    def on_device(matrix, band_cols, x_start, y_start, demand, scen_level, cost, upper, bound_type):
        row_blocks, band, blk, _ = matrix.shape
        rows, width = y_start.shape
        f32, bf16 = jnp.float32, jnp.bfloat16
        n_peers = C * R - 1
        dma = pltpu.SemaphoreType.DMA
        vmem = pl.BlockSpec(memory_space=pltpu.VMEM)
        anywhere = pl.BlockSpec(memory_space=pl.ANY)
        return pl.pallas_call(
            functools.partial(kernel, C, R),
            out_shape=(
                jax.ShapeDtypeStruct(x_start.shape, f32),
                jax.ShapeDtypeStruct(y_start.shape, f32),
                jax.ShapeDtypeStruct((2 * ITERS, width), f32),
            ),
            in_specs=[pl.BlockSpec(memory_space=pltpu.SMEM), anywhere, anywhere, anywhere,
                      vmem, vmem, vmem, vmem, vmem],
            out_specs=(anywhere, anywhere, vmem),
            scratch_shapes=[
                pltpu.VMEM(matrix.shape, bf16),
                pltpu.VMEM((3, rows, R * blk), bf16),
                pltpu.VMEM((3, rows, R * blk), bf16),
                pltpu.VMEM(x_start.shape, f32),
                pltpu.VMEM(y_start.shape, f32),
                pltpu.VMEM((rows, width), f32),
                pltpu.VMEM((width, rows), bf16),
                pltpu.VMEM((ITERS, 3, R, width, blk), f32),
                pltpu.VMEM((ITERS, 3, R, width, blk), f32),
                pltpu.VMEM((ITERS, 3, R, blk, width), bf16),
                pltpu.VMEM((4 * ITERS, width), f32),
                pltpu.VMEM((n_peers, 4 * ITERS, width), f32),
                dma((row_blocks,)),
                dma((2,)),
                dma((row_blocks + 1,)),
                dma((ITERS, 3, R)),
                dma((ITERS, 3, R)),
                dma((ITERS, 3, R)),
                dma((ITERS, 3, R)),
                dma((n_peers,)),
                dma((n_peers,)),
            ],
            compiler_params=pltpu.CompilerParams(
                collective_id=0, has_side_effects=True, vmem_limit_bytes=48 * 1024 * 1024
            ),
        )(band_cols, matrix, x_start, y_start, demand.T, scen_level.reshape(1, -1),
          cost.reshape(1, -1), upper.reshape(1, -1), bound_type.reshape(1, -1))

    placed = (
        P(("lp", "col", "row"), None, None, None),
        P(("lp", "col", "row"), None),
        P(("lp", "col", "row"), "sub"),
        P(("lp", "col", "row"), "sub"),
        P(("lp", "col", "row"), None),
        P(("lp", "sub")),
        P(("lp", "col", "row")),
        P(("lp", "col", "row")),
        P(("lp", "col", "row")),
    )
    return jax.shard_map(
        on_device,
        mesh=mesh,
        in_specs=placed,
        out_specs=(
            P(("lp", "col", "row"), "sub"),
            P(("lp", "col", "row"), "sub"),
            P(None, ("lp", "sub")),
        ),
        check_vma=False,
    )
```

time: 162 us -> 54.1 us (0.33)
  Pallas kernels: 0 us -> 43.3 us
  other arithmetic: 38.9 us -> 0 us
  waiting for transfers between devices: 33.5 us -> 0 us
  blocking collectives: 29.4 us -> 0 us
  starting transfers between devices: 14.4 us -> 0 us
  between operations: 14.3 us -> 0.66 us
  matrix products: 11.7 us -> 0 us
  local copies, waits for them, and re-layouts: 18.7 us -> 9.76 us
    pallas_call x0 -> x1, Pallas kernels: none -> 43.3 us  [on_device(): pl.pallas_call(functools.partial(kernel, C, R), out_shape=(jax.ShapeDtype...]
    scatter-add x2 -> x0, other arithmetic: 21.7 us -> none  [on_device(): jax.ops.segment_sum(products.reshape(row_blocks * band_size, block_size,...]
    psum x1 -> x0, blocking collectives: 20.3 us -> none  [on_device(): collected.append(lax.psum(partial_sums, ('col', 'row')))]
    ppermute x8 -> x0, waiting for transfers between devices: 20.2 us -> none  [from_behind(): lax.ppermute(value, axis, [(i, (i + by) % count) for i in range(count)])]
    ppermute x8 -> x0, starting transfers between devices: 14.3 us -> none  [from_behind(): lax.ppermute(value, axis, [(i, (i + by) % count) for i in range(count)])]
    reduce_scatter x2 -> x0, waiting for transfers between devices: 13.3 us -> none  [on_device(): pull_back = lax.psum_scatter(summed, 'row', scatter_dimension=0, tiled=True)]
    dot_general x5 -> x0, matrix products: 11.7 us -> none  [the longest x2 6.41 us: on_device(): jnp.einsum('ikab,ias->ikbs', matrix, dual.astype(jnp.bfloat16).reshape(ro...]
    reshape x3 -> x0, local copies, waits for them, and re-layouts: 10.1 us -> none  [the longest x1 5.96 us: on_device(): products.reshape(row_blocks * band_size, block_size, panel_width)]
  transfers between devices with their start and end apart: 10 -> 0, of which waited for: 10 -> 0; matrix products, arithmetic and copies ran while one was open for 2% -> 0% of each run, Pallas kernels for 0% -> 0%
where the time goes in v1:
time: 54.1 us; the launch traced here: 53.7 us
  Pallas kernels  43.3 us (80%)
  local copies, waits for them, and re-layouts  9.76 us (18%)
  between operations  0.66 us (1%)
    pallas_call x1, Pallas kernels, on_device(): pl.pallas_call(functools.partial(kernel, C, R), out_shape=(jax.ShapeDtype...  43.3 us
    unnamed x21, local copies, waits for them, and re-layouts  9.76 us

profile of v1, /device:TPU:0, one launch (start us, length us, event | category | flops | bytes accessed | tf_op | source)
XLA Modules:
  0.0 53.7 jit_solution(2429028403437928581)
XLA Ops:
  0.6 0.0 copy-start
  0.6 1.7 %copy-done = bf16[8,10,128,128]{3,2,1,0:T(8,128)(2,1)S(1)} copy-done((bf16[8,10,128,128]{3,2,1,0:T(8,128)(2,1)S(1)}, bf16[8,10,128,128]{3,2,1,0:T(8,128)(2,1)}, u32[]{:S(2)}) %copy-start) | copy-done | bytes 2621464
  2.4 0.0 copy-start.1
  2.4 1.0 %copy-done.1 = f32[1024,128]{1,0:T(8,128)S(1)} copy-done((f32[1024,128]{1,0:T(8,128)S(1)}, f32[1024,128]{1,0:T(8,128)}, u32[]{:S(2)}) %copy-start.1) | copy-done | bytes 524312
  3.4 0.0 copy-start.2
  3.4 0.8 %copy-done.2 = f32[128,128]{1,0:T(8,128)S(1)} copy-done((f32[128,128]{1,0:T(8,128)S(1)}, f32[128,128]{1,0:T(8,128)}, u32[]{:S(2)}) %copy-start.2) | copy-done | bytes 65560
  4.3 0.0 copy-start.3
  4.3 0.8 %copy-done.3 = f32[1024,16]{0,1:T(8,128)S(1)} copy-done((f32[1024,16]{0,1:T(8,128)S(1)}, f32[1024,16]{0,1:T(8,128)}, u32[]{:S(2)}) %copy-start.3) | copy-done | bytes 65560
  5.1 0.0 copy-start.4
  5.1 0.7 %copy-done.4 = s32[8,10]{1,0:T(8,128)S(1)} copy-done((s32[8,10]{1,0:T(8,128)S(1)}, s32[8,10]{1,0:T(8,128)}, u32[]{:S(2)}) %copy-start.4) | copy-done | bytes 344
  5.8 0.0 copy-start.5
  5.8 0.7 %copy-done.5 = s32[128]{0:T(128)S(1)} copy-done((s32[128]{0:T(128)S(1)}, s32[128]{0:T(128)}, u32[]{:S(2)}) %copy-start.5) | copy-done | bytes 536
  6.4 0.0 copy-start.6
  6.4 0.7 %copy-done.6 = f32[128]{0:T(128)S(1)} copy-done((f32[128]{0:T(128)S(1)}, f32[128]{0:T(128)}, u32[]{:S(2)}) %copy-start.6) | copy-done | bytes 536
  7.1 0.0 copy-start.7
  7.1 0.7 %copy-done.7 = f32[128]{0:T(128)S(1)} copy-done((f32[128]{0:T(128)S(1)}, f32[128]{0:T(128)}, u32[]{:S(2)}) %copy-start.7) | copy-done | bytes 536
  7.8 0.0 copy-start.8
  7.8 0.7 %copy-done.8 = s32[128]{0:T(128)S(1)} copy-done((s32[128]{0:T(128)S(1)}, s32[128]{0:T(128)}, u32[]{:S(2)}) %copy-start.8) | copy-done | bytes 536
  8.4 43.3 %shard_map.112 = (f32[128,128]{1,0:T(8,128)S(1)}, f32[1024,128]{1,0:T(8,128)S(1)}, f32[4,128]{1,0:T(4,128)S(1)}) custom-call(s32[8,10]{1,0:T(8,128)S(1)} %copy-done.4, bf16[8,10,128,128]{3,2,1,0:T(8,128)(2,1)S(1)} %copy-done, f32[128,128]{1,0:T(8,128)S(1)} %copy-done.2, f32[1024,128]{1,0:T(8,128)S(1)} %copy-done.1, f32[16,1024]{1,0:T(8,128)S(1)} %bitcast.5, ...), custom_call_target="tpu_custom_call" | custom-call | tf_op jit(solution)/shard_map/pallas_call | solution.py:221
  51.7 0.6 %copy.15 = f32[128,128]{1,0:T(8,128)} copy(f32[128,128]{1,0:T(8,128)S(1)} %get-tuple-element.6) | data formatting | bytes 131072
  52.3 0.8 %copy.16 = f32[1024,128]{1,0:T(8,128)} copy(f32[1024,128]{1,0:T(8,128)S(1)} %get-tuple-element.7) | data formatting | bytes 1048576
  53.1 0.6 %copy.17 = f32[4,128]{1,0:T(4,128)} copy(f32[4,128]{1,0:T(4,128)S(1)} %get-tuple-element.8) | data formatting | bytes 4096
Async XLA Ops:
  0.6 1.7 %copy-start = (bf16[8,10,128,128]{3,2,1,0:T(8,128)(2,1)S(1)}, bf16[8,10,128,128]{3,2,1,0:T(8,128)(2,1)}, u32[]{:S(2)}) copy-start(bf16[8,10,128,128]{3,2,1,0:T(8,128)(2,1)} %mat_hbm.1) | copy-start | bytes 7864324
  2.4 1.0 %copy-start.1 = (f32[1024,128]{1,0:T(8,128)S(1)}, f32[1024,128]{1,0:T(8,128)}, u32[]{:S(2)}) copy-start(f32[1024,128]{1,0:T(8,128)} %y_hbm.1) | copy-start | bytes 1572868
  3.4 0.8 %copy-start.2 = (f32[128,128]{1,0:T(8,128)S(1)}, f32[128,128]{1,0:T(8,128)}, u32[]{:S(2)}) copy-start(f32[128,128]{1,0:T(8,128)} %x_hbm.1) | copy-start | bytes 196612
  4.3 0.8 %copy-start.3 = (f32[1024,16]{0,1:T(8,128)S(1)}, f32[1024,16]{0,1:T(8,128)}, u32[]{:S(2)}) copy-start(f32[1024,16]{0,1:T(8,128)} %param.13) | copy-start | bytes 196612
  5.1 0.7 %copy-start.4 = (s32[8,10]{1,0:T(8,128)S(1)}, s32[8,10]{1,0:T(8,128)}, u32[]{:S(2)}) copy-start(s32[8,10]{1,0:T(8,128)} %cols_ref.1) | copy-start | bytes 964
  5.8 0.7 %copy-start.5 = (s32[128]{0:T(128)S(1)}, s32[128]{0:T(128)}, u32[]{:S(2)}) copy-start(s32[128]{0:T(128)} %param.14) | copy-start | bytes 1540
  6.4 0.7 %copy-start.6 = (f32[128]{0:T(128)S(1)}, f32[128]{0:T(128)}, u32[]{:S(2)}) copy-start(f32[128]{0:T(128)} %param.15) | copy-start | bytes 1540
  7.1 0.7 %copy-start.7 = (f32[128]{0:T(128)S(1)}, f32[128]{0:T(128)}, u32[]{:S(2)}) copy-start(f32[128]{0:T(128)} %param.16) | copy-start | bytes 1540
  7.8 0.7 %copy-start.8 = (s32[128]{0:T(128)S(1)}, s32[128]{0:T(128)}, u32[]{:S(2)}) copy-start(s32[128]{0:T(128)} %param.17) | copy-start | bytes 1540

commit v2 on v1

--- a/solution.py
+++ b/solution.py
@@ -13,43 +13,71 @@
 eps = 1e-06
 MESH = pl.DeviceIdType.MESH
 CHUNK = 32
+EXTRA = 16
+
+
+def coded(block):
+    most = jnp.max(jnp.abs(block), axis=0, keepdims=True)
+    power = jnp.ceil(jnp.log2(jnp.maximum(most, 1e-30)))
+    units = jnp.minimum(jnp.round(block * jnp.exp2(15.0 - power)), 32767.0)
+    powers = jnp.broadcast_to(power, (EXTRA, block.shape[1]))
+    return jnp.concatenate([units, powers], axis=0).astype(jnp.int32).astype(jnp.int16)
+
+
+def decoded(message):
+    values = message.astype(jnp.int32).astype(jnp.float32)
+    return values[:-EXTRA] * jnp.exp2(values[-EXTRA:][:1] - 15.0)
 
 
 def dot(a, b):
     return jnp.dot(a, b, preferred_element_type=jnp.float32)
 
 
-def kernel(C, R, cols_ref, mat_hbm, x_hbm, y_hbm, dem_ref, level_ref, cost_ref, upper_ref, kind_ref,
+def kernel(C, R, cols_hbm, mat_hbm, x_hbm, y_hbm, dem_hbm, level_hbm, cost_hbm, upper_hbm, kind_hbm,
            x_out, y_out, score_ref,
-           mat, hi, lo, xv, yv, panel, dual_t, pbuf, rbuf, xbuf, sums, others,
+           cols_ref, dem_ref, level_ref, cost_ref, upper_ref, kind_ref, mat, hi, lo, own, xv, yv, panel, dual_t, pbuf, rbuf, xbuf, sums, others,
            mat_sem, in_sem, out_sem, p_send, p_recv, x_send, x_recv, s_send, s_recv):
     row_blocks, band, blk, _ = mat.shape
     rows = row_blocks * blk
     levels = dem_ref.shape[0]
     ci, ri = lax.axis_index("col"), lax.axis_index("row")
 
+    def ring(at, by, size):
+        at = at + by % size
+        return jnp.where(at >= size, at - size, at)
+
     def peer(dc, dr):
-        return {"col": lax.rem(ci + dc + C, C), "row": lax.rem(ri + dr, R)}
+        return {"col": ring(ci, dc, C), "row": ring(ri, dr, R)}
 
     peers = [(dc, dr) for dc in range(C) for dr in range(R) if (dc, dr) != (0, 0)]
+
+    barrier = pltpu.get_barrier_semaphore()
+    for dc, dr in peers:
+        pl.semaphore_signal(barrier, inc=1, device_id=peer(dc, dr), device_id_type=MESH)
 
     y_in = pltpu.make_async_copy(y_hbm, yv, in_sem.at[0])
     x_in = pltpu.make_async_copy(x_hbm, xv, in_sem.at[1])
 
+    small_in = [
+        pltpu.make_async_copy(a, b, in_sem.at[2 + n]) for n, (a, b) in enumerate((
+            (cols_hbm, cols_ref), (dem_hbm, dem_ref), (level_hbm, level_ref),
+            (cost_hbm, cost_ref), (upper_hbm, upper_ref), (kind_hbm, kind_ref)))]
+
     def mat_in(i):
         return pltpu.make_async_copy(mat_hbm.at[i], mat.at[i], mat_sem.at[i])
 
+    small_in[0].start()
     mat_in(0).start()
     y_in.start()
     x_in.start()
     for i in range(1, row_blocks):
         mat_in(i).start()
-
-    barrier = pltpu.get_barrier_semaphore()
-    for dc, dr in peers:
-        pl.semaphore_signal(barrier, inc=1, device_id=peer(dc, dr), device_id_type=MESH)
-
-    slot_col = [lax.rem(ci + s - 1 + C, C) * R + w for s in range(3) for w in range(R)]
+    for copy in small_in[1:]:
+        copy.start()
+
+    slot_col = [ring(ci, s - 1, C) * R + w for s in range(3) for w in range(R)]
+
+    small_in[0].wait()
 
     def densify(i, carry):
         mat_in(i).wait()
@@ -84,7 +112,7 @@
     pl.semaphore_wait(barrier, len(peers))
 
     def down(t, s, dr):
-        w = lax.rem(ri + dr, R)
+        w = ring(ri, dr, R)
         return pltpu.make_async_remote_copy(
             src_ref=pbuf.at[t, s, w], dst_ref=rbuf.at[t, s, dr],
             send_sem=p_send.at[t, s, dr], recv_sem=p_recv.at[t, s, dr],
@@ -97,7 +125,7 @@
             device_id=peer(1 - s, dr), device_id_type=MESH)
 
     def arrival(t, s, dr):
-        w = lax.rem(ri - dr + R, R)
+        w = ring(ri, -dr, R)
         return pltpu.make_async_remote_copy(
             src_ref=xbuf.at[t, 1, ri], dst_ref=xbuf.at[t, s, w],
             send_sem=x_send.at[t, s, dr], recv_sem=x_recv.at[t, s, dr],
@@ -110,12 +138,17 @@
         for s in (0, 2, 1):
             product = dot(d, hi[s]) + dot(d, lo[s])
             for w in range(R):
-                pbuf[t, s, w] = product[:, w * blk:(w + 1) * blk]
+                block = product[:, w * blk:(w + 1) * blk]
+                if s == 1:
+                    own[w] = block
+                pbuf[t, s, w] = coded(block)
             for dr in range(R):
                 if (s, dr) != (1, 0):
                     down(t, s, dr).start()
         if t == 0:
             x_in.wait()
+            for copy in small_in[1:]:
+                copy.wait()
             rows_of = lax.broadcasted_iota(jnp.int32, (levels, blk), 0)
             pick = jnp.where(rows_of == level_ref[...], 1.0, 0.0).astype(jnp.bfloat16)
             part_1 = dem_ref[...].astype(jnp.bfloat16)
@@ -129,10 +162,10 @@
             cost = jnp.broadcast_to(cost_ref[...], (blk, blk)).T
             upper = jnp.broadcast_to(upper_ref[...], (blk, blk)).T
             kind = jnp.broadcast_to(kind_ref[...], (blk, blk)).astype(jnp.float32).T
-        pulled = pbuf[t, 1, ri]
+        pulled = own[ri]
         for s, dr in moves[::-1]:
             down(t, s, dr).wait_recv()
-            pulled = pulled + rbuf[t, s, dr]
+            pulled = pulled + decoded(rbuf[t, s, dr])
         primal = xv[...]
         value = primal - step_primal * (cost - pulled.T)
         low = jnp.maximum(value, 0.0)
@@ -207,6 +240,22 @@
         copy.wait()
 
 
+def store(x_ref, y_ref, score_ref, x_out, y_out, score_out, x_at, y_at, score_at, sem):
+    part = y_ref.shape[0] // 4
+    trips = [(r.at[i * part:(i + 1) * part], y_at.at[i * part:(i + 1) * part], o.at[i * part:(i + 1) * part])
+             for i in range(4) for r, o in [(y_ref, y_out)]]
+    trips += [(x_ref, x_at, x_out), (score_ref, score_at, score_out)]
+    loads = [pltpu.make_async_copy(a, b, sem.at[0, n]) for n, (a, b, _) in enumerate(trips)]
+    stores = [pltpu.make_async_copy(b, c, sem.at[1, n]) for n, (_, b, c) in enumerate(trips)]
+    for copy in loads:
+        copy.start()
+    for load, copy in zip(loads, stores):
+        load.wait()
+        copy.start()
+    for copy in stores:
+        copy.wait()
+
+
 def solution(mesh):
     C, R = mesh.shape["col"], mesh.shape["row"]
 
@@ -218,31 +267,38 @@
         dma = pltpu.SemaphoreType.DMA
         vmem = pl.BlockSpec(memory_space=pltpu.VMEM)
         anywhere = pl.BlockSpec(memory_space=pl.ANY)
-        return pl.pallas_call(
+        shapes = (
+            jax.ShapeDtypeStruct(x_start.shape, f32),
+            jax.ShapeDtypeStruct(y_start.shape, f32),
+            jax.ShapeDtypeStruct((2 * ITERS, width), f32),
+        )
+        results = pl.pallas_call(
             functools.partial(kernel, C, R),
-            out_shape=(
-                jax.ShapeDtypeStruct(x_start.shape, f32),
-                jax.ShapeDtypeStruct(y_start.shape, f32),
-                jax.ShapeDtypeStruct((2 * ITERS, width), f32),
-            ),
-            in_specs=[pl.BlockSpec(memory_space=pltpu.SMEM), anywhere, anywhere, anywhere,
-                      vmem, vmem, vmem, vmem, vmem],
+            out_shape=shapes,
+            in_specs=[pl.BlockSpec(memory_space=pltpu.HBM)] * 9,
             out_specs=(anywhere, anywhere, vmem),
             scratch_shapes=[
+                pltpu.SMEM(band_cols.shape, jnp.int32),
+                pltpu.VMEM(demand.shape[::-1], f32),
+                pltpu.VMEM((1, width), jnp.int32),
+                pltpu.VMEM((1, blk), f32),
+                pltpu.VMEM((1, blk), f32),
+                pltpu.VMEM((1, blk), jnp.int32),
                 pltpu.VMEM(matrix.shape, bf16),
                 pltpu.VMEM((3, rows, R * blk), bf16),
                 pltpu.VMEM((3, rows, R * blk), bf16),
+                pltpu.VMEM((R, width, blk), f32),
                 pltpu.VMEM(x_start.shape, f32),
                 pltpu.VMEM(y_start.shape, f32),
                 pltpu.VMEM((rows, width), f32),
                 pltpu.VMEM((width, rows), bf16),
-                pltpu.VMEM((ITERS, 3, R, width, blk), f32),
-                pltpu.VMEM((ITERS, 3, R, width, blk), f32),
+                pltpu.VMEM((ITERS, 3, R, width + EXTRA, blk), jnp.int16),
+                pltpu.VMEM((ITERS, 3, R, width + EXTRA, blk), jnp.int16),
                 pltpu.VMEM((ITERS, 3, R, blk, width), bf16),
                 pltpu.VMEM((4 * ITERS, width), f32),
                 pltpu.VMEM((n_peers, 4 * ITERS, width), f32),
                 dma((row_blocks,)),
-                dma((2,)),
+                dma((8,)),
                 dma((row_blocks + 1,)),
                 dma((ITERS, 3, R)),
                 dma((ITERS, 3, R)),
@@ -252,10 +308,18 @@
                 dma((n_peers,)),
             ],
             compiler_params=pltpu.CompilerParams(
-                collective_id=0, has_side_effects=True, vmem_limit_bytes=48 * 1024 * 1024
+                collective_id=0, has_side_effects=True, vmem_limit_bytes=62 * 1024 * 1024
             ),
         )(band_cols, matrix, x_start, y_start, demand.T, scen_level.reshape(1, -1),
           cost.reshape(1, -1), upper.reshape(1, -1), bound_type.reshape(1, -1))
+        return pl.pallas_call(
+            store,
+            out_shape=shapes,
+            in_specs=[anywhere] * 3,
+            out_specs=(anywhere,) * 3,
+            scratch_shapes=[pltpu.VMEM(q.shape, f32) for q in shapes] + [dma((2, 6))],
+            compiler_params=pltpu.CompilerParams(vmem_limit_bytes=62 * 1024 * 1024),
+        )(*results)
 
     placed = (
         P(("lp", "col", "row"), None, None, None),

time: 54.1 us -> 42.2 us (0.78)
  local copies, waits for them, and re-layouts: 9.76 us -> 0 us
  Pallas kernels: 43.3 us -> 41.4 us
    unnamed x21 -> x0, local copies, waits for them, and re-layouts: 9.76 us -> none
    pallas_call x1 -> x2, Pallas kernels: 43.3 us -> 41.4 us  [the longest x1 39.5 us: on_device(): pl.pallas_call(functools.partial(kernel, C, R), out_shape=shapes, in_spec...]
where the time goes in v2:
time: 42.2 us; the launch traced here: 42.1 us
  Pallas kernels  41.4 us (98%)
  between operations  0.64 us (2%)
    pallas_call x1, Pallas kernels, on_device(): pl.pallas_call(functools.partial(kernel, C, R), out_shape=shapes, in_spec...  39.5 us
    pallas_call x1, Pallas kernels, on_device(): pl.pallas_call(store, out_shape=shapes, in_specs=[anywhere] * 3, out_spec...  1.87 us

profile of v2, /device:TPU:0, one launch (start us, length us, event | category | flops | bytes accessed | tf_op | source)
XLA Modules:
  0.0 42.1 jit_solution(1040387783166382495)
XLA Ops:
  0.6 39.5 %shard_map.112 = (f32[128,128]{1,0:T(8,128)}, f32[1024,128]{1,0:T(8,128)}, f32[4,128]{1,0:T(4,128)}) custom-call(s32[8,10]{1,0:T(8,128)} %cols_hbm.1, bf16[8,10,128,128]{3,2,1,0:T(8,128)(2,1)} %mat_hbm.1, f32[128,128]{1,0:T(8,128)} %x_hbm.1, f32[1024,128]{1,0:T(8,128)} %y_hbm.1, f32[16,1024]{1,0:T(8,128)} %bitcast.5, s32[1,128]{1,0:T(1,128)} %bitcast.6, ...), custom_call_target="tpu_custom_call" | custom-call | tf_op jit(solution)/shard_map/pallas_call | solution.py:275
  40.2 1.9 %shard_map.113 = (f32[128,128]{1,0:T(8,128)}, f32[1024,128]{1,0:T(8,128)}, f32[4,128]{1,0:T(4,128)}) custom-call(f32[128,128]{1,0:T(8,128)} %get-tuple-element.6.x_ref, f32[1024,128]{1,0:T(8,128)} %get-tuple-element.7.y_ref, f32[4,128]{1,0:T(4,128)} %get-tuple-element.8.score_ref), custom_call_target="tpu_custom_call" | custom-call | tf_op jit(solution)/shard_map/pallas_call | solution.py:315

commit v3 on v2

--- a/solution.py
+++ b/solution.py
@@ -12,7 +12,7 @@
 step_dual = 0.3
 eps = 1e-06
 MESH = pl.DeviceIdType.MESH
-CHUNK = 32
+CHUNK = 64
 EXTRA = 16
 
 
@@ -79,37 +79,37 @@
 
     small_in[0].wait()
 
-    def densify(i, carry):
-        mat_in(i).wait()
-        marks = []
-        for k in range(band):
-            col = cols_ref[i, k]
-            marks.append([jnp.where(col == c, 1.0, 0.0).astype(jnp.float32) for c in slot_col])
-
-        def part(r, carry):
-            at = pl.ds(pl.multiple_of(r * CHUNK, CHUNK), CHUNK)
-            to = pl.ds(pl.multiple_of(i * blk + r * CHUNK, CHUNK), CHUNK)
-            total = [None] * (3 * R)
+    def densify(s, first):
+        def one(i, carry):
+            if first:
+                mat_in(i).wait()
+            marks = []
             for k in range(band):
-                tile = mat[i, k, at, :].astype(jnp.float32)
-                for j in range(3 * R):
-                    term = marks[k][j] * tile
-                    total[j] = term if k == 0 else total[j] + term
-            for j in range(3 * R):
-                s, w = j // R, j % R
-                top = total[j].astype(jnp.bfloat16)
-                hi[s, to, w * blk:(w + 1) * blk] = top
-                lo[s, to, w * blk:(w + 1) * blk] = (total[j] - top.astype(jnp.float32)).astype(jnp.bfloat16)
-            return carry
-
-        return lax.fori_loop(0, blk // CHUNK, part, carry)
-
-    lax.fori_loop(0, row_blocks, densify, 0)
+                col = cols_ref[i, k]
+                marks.append([jnp.where(col == c, 1.0, 0.0).astype(jnp.float32) for c in slot_col[s * R:(s + 1) * R]])
+
+            def part(r, carry):
+                at = pl.ds(pl.multiple_of(r * CHUNK, CHUNK), CHUNK)
+                to = pl.ds(pl.multiple_of(i * blk + r * CHUNK, CHUNK), CHUNK)
+                total = [None] * R
+                for k in range(band):
+                    tile = mat[i, k, at, :].astype(jnp.float32)
+                    for w in range(R):
+                        term = marks[k][w] * tile
+                        total[w] = term if k == 0 else total[w] + term
+                for w in range(R):
+                    top = total[w].astype(jnp.bfloat16)
+                    hi[s, to, w * blk:(w + 1) * blk] = top
+                    lo[s, to, w * blk:(w + 1) * blk] = (total[w] - top.astype(jnp.float32)).astype(jnp.bfloat16)
+                return carry
+
+            return lax.fori_loop(0, blk // CHUNK, part, carry, unroll=True)
+
+        lax.fori_loop(0, row_blocks, one, 0)
 
     y_in.wait()
     for i in range(row_blocks):
         dual_t[:, i * blk:(i + 1) * blk] = yv[i * blk:(i + 1) * blk, :].T.astype(jnp.bfloat16)
-    pl.semaphore_wait(barrier, len(peers))
 
     def down(t, s, dr):
         w = ring(ri, dr, R)
@@ -136,12 +136,16 @@
     for t in range(ITERS):
         d = dual_t[...]
         for s in (0, 2, 1):
+            if t == 0:
+                densify(s, s == 0)
             product = dot(d, hi[s]) + dot(d, lo[s])
             for w in range(R):
                 block = product[:, w * blk:(w + 1) * blk]
                 if s == 1:
                     own[w] = block
                 pbuf[t, s, w] = coded(block)
+            if (t, s) == (0, 0):
+                pl.semaphore_wait(barrier, len(peers))
             for dr in range(R):
                 if (s, dr) != (1, 0):
                     down(t, s, dr).start()

time: 42.2 us -> 39.2 us (0.929)
  Pallas kernels: 41.4 us -> 38.4 us
    pallas_call x1, Pallas kernels: 39.5 us -> 36.5 us  [on_device(): pl.pallas_call(functools.partial(kernel, C, R), out_shape=shapes, in_spec...]
where the time goes in v3:
time: 39.2 us; the launch traced here: 39 us
  Pallas kernels  38.4 us (98%)
  between operations  0.64 us (2%)
    pallas_call x1, Pallas kernels, on_device(): pl.pallas_call(functools.partial(kernel, C, R), out_shape=shapes, in_spec...  36.5 us
    pallas_call x1, Pallas kernels, on_device(): pl.pallas_call(store, out_shape=shapes, in_specs=[anywhere] * 3, out_spec...  1.87 us

profile of v3, /device:TPU:0, one launch (start us, length us, event | category | flops | bytes accessed | tf_op | source)
XLA Modules:
  0.0 39.0 jit_solution(7497743290683779544)
XLA Ops:
  0.6 36.5 %shard_map.112 = (f32[128,128]{1,0:T(8,128)}, f32[1024,128]{1,0:T(8,128)}, f32[4,128]{1,0:T(4,128)}) custom-call(s32[8,10]{1,0:T(8,128)} %cols_hbm.1, bf16[8,10,128,128]{3,2,1,0:T(8,128)(2,1)} %mat_hbm.1, f32[128,128]{1,0:T(8,128)} %x_hbm.1, f32[1024,128]{1,0:T(8,128)} %y_hbm.1, f32[16,1024]{1,0:T(8,128)} %bitcast.5, s32[1,128]{1,0:T(1,128)} %bitcast.6, ...), custom_call_target="tpu_custom_call" | custom-call | tf_op jit(solution)/shard_map/pallas_call | solution.py:279
  37.2 1.9 %shard_map.113 = (f32[128,128]{1,0:T(8,128)}, f32[1024,128]{1,0:T(8,128)}, f32[4,128]{1,0:T(4,128)}) custom-call(f32[128,128]{1,0:T(8,128)} %get-tuple-element.6.x_ref, f32[1024,128]{1,0:T(8,128)} %get-tuple-element.7.y_ref, f32[4,128]{1,0:T(4,128)} %get-tuple-element.8.score_ref), custom_call_target="tpu_custom_call" | custom-call | tf_op jit(solution)/shard_map/pallas_call | solution.py:319
